TPU v7x, 256 devices: a whole 4x4x8 slice. The times are simulated.
256 devices in a mesh: dp: 8 (over y, z_hi), center: 32 (over z_lo, x, core).
Axes of the slice: x: 4, y: 4, z: 8 (z_hi: 2, z_lo: 4; z = z_hi * 4 + z_lo), core: 2. Of those that a mesh axis runs over, the one named last changes fastest.
Arguments:
- embeddings: bfloat16 [8192, 2048], P('dp', 'center'), may hold values from -6 to 6
- first_weight: bfloat16 [2048, 2048], P(None, 'center'), may hold values from -0.125 to 0.125
- first_bias: float32 [2048], P('center'), may hold values from -3 to 3
- second_weight: bfloat16 [2048, 512], P('center'), may hold values from -0.1875 to 0.1875
- centers: bfloat16 [65536, 512], P('center'), may hold values from -4 to 4
- coefficients: bfloat16 [65536, 100], P('center'), may hold values from -12 to 12
- cotangent: bfloat16 [8192, 100], P('dp'), may hold values from -18 to 18
Outputs:
- predictions: float32 [8192, 100], P(('dp', 'center'))
- grad_first: float32 [2048, 2048], P('dp', 'center')
- grad_bias: float32 [2048], P('center')
- grad_second: float32 [2048, 512], P('center', 'dp')
- grad_centers: float32 [65536, 512], P('center', 'dp')
- grad_coefs: float32 [65536, 100], P('center')
All inputs are finite; a program needn't handle non-finite values.
Results may differ from a plain program's by a relative error of at most 0.028.
Values may be sent and summed in bfloat16 or wider, within the bound.
A program may use at most 64 MiB of HBM per device.

v0:
```python
import jax
import jax.numpy as jnp
from jax import lax
from jax.sharding import PartitionSpec as P


def body(embeddings, first_weight, first_bias, second_weight, centers, coefficients, cotangent):
    feat_width = centers.shape[1]
    factor = 16.0 / feat_width
    gathered = lax.all_gather(embeddings, "center", axis=1, tiled=True)
    preact = jnp.dot(gathered, first_weight, preferred_element_type=jnp.float32) + first_bias
    hidden = jax.nn.gelu(preact).astype(jnp.bfloat16)
    feature_sum = lax.psum(
        jnp.dot(hidden, second_weight, preferred_element_type=jnp.float32), "center"
    )
    squashed = jnp.tanh(feature_sum)
    features = squashed.astype(jnp.bfloat16)
    feat_wide = features.astype(jnp.float32)
    center_wide = centers.astype(jnp.float32)
    feat_norms = jnp.sum(feat_wide * feat_wide, axis=1)
    center_norms = jnp.sum(center_wide * center_wide, axis=1)
    inner_prods = jnp.einsum("tf,cf->tc", features, centers, preferred_element_type=jnp.float32)
    sq_dist = feat_norms[:, None] + center_norms[None, :] - 2.0 * inner_prods
    kernel = jnp.exp(-8.0 * sq_dist / feat_width).astype(jnp.bfloat16)
    pred_part = jnp.dot(kernel, coefficients, preferred_element_type=jnp.float32)
    kernel_grad = jnp.einsum(
        "to,co->tc", cotangent, coefficients, preferred_element_type=jnp.float32
    )
    weighted = kernel_grad * kernel.astype(jnp.float32)
    weighted_low = weighted.astype(jnp.bfloat16)
    feat_grad_part = -factor * (
        jnp.sum(weighted, axis=1)[:, None] * feat_wide
        - jnp.dot(weighted_low, centers, preferred_element_type=jnp.float32)
    )
    center_grad = -factor * (
        jnp.sum(weighted, axis=0)[:, None] * center_wide
        - jnp.einsum("tc,tf->cf", weighted_low, features, preferred_element_type=jnp.float32)
    )
    coef_grad = jnp.einsum("tc,to->co", kernel, cotangent, preferred_element_type=jnp.float32)
    predictions = lax.psum_scatter(
        pred_part.astype(jnp.bfloat16), "center", scatter_dimension=0, tiled=True
    ).astype(jnp.float32)
    feature_grad = lax.psum(feat_grad_part.astype(jnp.bfloat16), "center").astype(jnp.float32)
    phi_grad = (feature_grad * (1.0 - squashed * squashed)).astype(jnp.bfloat16)
    second_grad = jnp.einsum("th,tf->hf", hidden, phi_grad, preferred_element_type=jnp.float32)
    hidden_grad = jnp.einsum(
        "tf,hf->th", phi_grad, second_weight, preferred_element_type=jnp.float32
    )
    unused, pullback = jax.vjp(jax.nn.gelu, preact)
    preact_grad = pullback(hidden_grad)[0]
    bias_grad = jnp.sum(preact_grad, axis=0)
    preact_low = preact_grad.astype(jnp.bfloat16)
    first_grad = jnp.einsum("ti,th->ih", gathered, preact_low, preferred_element_type=jnp.float32)
    first_grad, second_grad, center_grad = (
        lax.psum_scatter(
            first_grad.astype(jnp.bfloat16), "dp", scatter_dimension=0, tiled=True
        ).astype(jnp.float32),
        lax.psum_scatter(
            second_grad.astype(jnp.bfloat16), "dp", scatter_dimension=1, tiled=True
        ).astype(jnp.float32),
        lax.psum_scatter(
            center_grad.astype(jnp.bfloat16), "dp", scatter_dimension=1, tiled=True
        ).astype(jnp.float32),
    )
    bias_grad, coef_grad = (
        lax.psum(bias_grad.astype(jnp.bfloat16), "dp").astype(jnp.float32),
        lax.psum(coef_grad.astype(jnp.bfloat16), "dp").astype(jnp.float32),
    )
    return (predictions, first_grad, bias_grad, second_grad, center_grad, coef_grad)


def solution(mesh):
    placed = (
        P("dp", "center"),
        P(None, "center"),
        P("center"),
        P("center", None),
        P("center", None),
        P("center", None),
        P("dp", None),
    )
    return jax.shard_map(
        body,
        mesh=mesh,
        in_specs=placed,
        out_specs=(
            P(("dp", "center"), None),
            P("dp", "center"),
            P("center"),
            P("center", "dp"),
            P("center", "dp"),
            P("center", None),
        ),
        check_vma=False,
    )
```

profile of v0, /device:TPU:1, one launch (start us, length us, event | category | flops | bytes accessed | tf_op | source)
XLA Modules:
  0.0 1175.9 jit_solution(6717297823723583813)
XLA Ops:
  7.2 0.0 all-gather.2.cloned.1.call-start
  7.2 0.7 all-gather.2.cloned.1.call-update
  7.9 0.0 all-reduce.4.cloned.1.call-start
  8.0 69.1 %all-gather.2.cloned.1.call-done = bf16[1024,2048]{0,1:T(8,128)(2,1)} async-done(((bf16[1024,64]{0,1:T(8,128)(2,1)}), bf16[1024,2048]{0,1:T(8,128)(2,1)}) %all-gather.2.cloned.1.call-update) | async-done | bytes 4194320 | tf_op jit(solution)/shard_map/all_gather | solution.py:10
  77.0 3.1 convolution_add_fusion
  80.1 1.8 fusion.21
  81.9 0.0 all-reduce.4.cloned.1.call-update
  82.0 0.0 all-reduce.6.cloned.1.call-start
  82.0 2.9 copy.14
  84.9 0.5 fusion
  85.4 276.7 %all-reduce.4.cloned.1.call-done = f32[1024,512]{1,0:T(8,128)} async-done(((f32[1024,512]{1,0:T(8,128)}), f32[1024,512]{1,0:T(8,128)}) %all-reduce.4.cloned.1.call-update) | async-done | bytes 2097168 | tf_op jit(solution)/shard_map/psum | solution.py:13
  362.1 2.0 fusion.5
  364.1 4.9 exponential_convert_fusion
  369.1 1.7 fusion.22
  370.8 0.4 copy-done.1
  371.2 2.0 copy-done.7
  373.2 3.4 fusion.8
  376.6 0.0 reduce-scatter.7.cloned.1.call-start
  376.6 4.1 convolution_convert_fusion.2
  380.8 0.0 reduce-scatter.7.cloned.1.call-update
  380.8 0.0 all-reduce.8.cloned.1.call-start
  380.9 3.7 convolution_convert_fusion
  384.6 0.0 all-reduce.8.cloned.1.call-update
  384.6 0.0 reduce-scatter.13.cloned.1.call-start
  384.7 268.8 %all-reduce.6.cloned.1.call-done = bf16[1024,512]{1,0:T(8,128)(2,1)} async-done(((bf16[1024,512]{1,0:T(8,128)(2,1)}), bf16[1024,512]{1,0:T(8,128)(2,1)}) %all-reduce.6.cloned.1.call-update) | async-done | bytes 1048592 | tf_op jit(solution)/shard_map/psum | solution.py:43
  653.4 2.4 multiply_convert_fusion
  655.8 1.1 copy-done.2
  656.9 0.3 convolution_convert_fusion.3
  657.2 0.8 copy.15
  658.0 1.8 fusion.23
  659.8 0.0 reduce-scatter.13.cloned.1.call-update
  659.8 0.0 reduce-scatter.9.cloned.1.call-start
  659.8 4.3 fusion.4
  664.2 0.2 reduce-scatter.11.cloned.1.call-start
  664.4 6.5 fusion.3
  670.9 123.0 %reduce-scatter.7.cloned.1.call-done = bf16[32,100]{1,0:T(8,128)(2,1)} async-done(((bf16[1024,100]{1,0:T(8,128)(2,1)}), bf16[32,100]{1,0:T(8,128)(2,1)}) %reduce-scatter.7.cloned.1.call-update) | async-done | bytes 6416 | tf_op jit(solution)/shard_map/reduce_scatter | solution.py:40
  793.9 1.3 convert_element_type.78
  795.2 107.3 %all-reduce.8.cloned.1.call-done = bf16[2048,100]{0,1:T(8,128)(2,1)} async-done(((bf16[2048,100]{0,1:T(8,128)(2,1)}), bf16[2048,100]{0,1:T(8,128)(2,1)}) %all-reduce.8.cloned.1.call-update) | async-done | bytes 409616 | tf_op jit(solution)/shard_map/psum | solution.py:67
  902.5 2.0 convert_element_type.95
  904.5 21.5 %psum.30 = bf16[64]{0:T(256)(128)(2,1)S(1)} all-reduce(bf16[64]{0:T(256)(128)(2,1)S(1)} %get-tuple-element.8), channel_id=1, replica_groups=mesh['dp'=8,'center'=32] {'dp'}, use_global_device_ids=true, to_apply=%region_8.0 | all-reduce | flops 64 | bytes 256 | tf_op jit(solution)/shard_map/psum | solution.py:66
  926.1 0.5 convert_element_type.89
  926.6 60.7 %reduce-scatter.13.cloned.1.call-done = bf16[64,64]{1,0:T(8,128)(2,1)} async-done(((bf16[512,64]{1,0:T(8,128)(2,1)}), bf16[64,64]{1,0:T(8,128)(2,1)}) %reduce-scatter.13.cloned.1.call-update) | async-done | bytes 8208
  987.3 0.8 copy.16
  988.1 0.6 convert_element_type.91
  988.7 81.8 %reduce-scatter.9.cloned.1.call-done = bf16[256,64]{0,1:T(8,128)(2,1)} async-done(((bf16[2048,64]{0,1:T(8,128)(2,1)}), bf16[256,64]{0,1:T(8,128)(2,1)}) %reduce-scatter.9.cloned.1.call-update) | async-done | bytes 32784 | tf_op jit(solution)/shard_map/reduce_scatter | solution.py:55
  1070.5 1.4 convert_element_type.87
  1071.9 95.4 %reduce-scatter.11.cloned.1.call-done = bf16[2048,64]{0,1:T(8,128)(2,1)} async-done(((bf16[2048,512]{0,1:T(8,128)(2,1)}), bf16[2048,64]{0,1:T(8,128)(2,1)}) %reduce-scatter.11.cloned.1.call-update) | async-done | bytes 262160 | tf_op jit(solution)/shard_map/reduce_scatter | solution.py:61
  1167.3 1.8 convert_element_type.93
  (16 shorter events, 0.1 us)
Async XLA Ops:
  7.2 361.9 %copy-start = (bf16[2048,100]{0,1:T(8,128)(2,1)S(1)}, bf16[2048,100]{0,1:T(8,128)(2,1)}, u32[]{:S(2)}) copy-start(bf16[2048,100]{0,1:T(8,128)(2,1)} %param.12) | copy-start | bytes 1228804
  7.2 72.9 %copy-start.6 = (bf16[64,512]{1,0:T(8,128)(2,1)S(1)}, bf16[64,512]{1,0:T(8,128)(2,1)}, u32[]{:S(2)}) copy-start(bf16[64,512]{1,0:T(8,128)(2,1)} %param.10) | copy-start | bytes 196612
  7.2 69.9 %all-gather.2.cloned.1.call-start = ((), (), s32[]{:S(2)}) async-start(), calls=%async_computation.4 | async-start | bytes 4325376 | tf_op jit(solution)/shard_map/all_gather | solution.py:10
  7.9 354.2 %all-reduce.4.cloned.1.call-start = ((), (), s32[]{:S(2)}) async-start(), calls=%async_computation.5 | async-start | bytes 4194304 | tf_op jit(solution)/shard_map/psum | solution.py:13
  82.0 571.5 %all-reduce.6.cloned.1.call-start = ((), (), s32[]{:S(2)}) async-start(), calls=%async_computation.7 | async-start | bytes 2097152 | tf_op jit(solution)/shard_map/psum | solution.py:43
  364.1 7.1 copy-start.4
  364.1 5.0 copy-start.5
  369.1 2.1 copy-start.1
  369.1 4.1 copy-start.3
  371.2 2.0 copy-start.7
  376.6 417.3 %reduce-scatter.7.cloned.1.call-start = ((), (), s32[]{:S(2)}) async-start(), calls=%async_computation.6 | async-start | bytes 270336 | tf_op jit(solution)/shard_map/reduce_scatter | solution.py:40
  380.8 521.7 %all-reduce.8.cloned.1.call-start = ((), (), s32[]{:S(2)}) async-start(), calls=%async_computation.10 | async-start | bytes 851968 | tf_op jit(solution)/shard_map/psum | solution.py:67
  384.6 602.7 %reduce-scatter.13.cloned.1.call-start = ((), (), s32[]{:S(2)}) async-start(), calls=%async_computation.11 | async-start | bytes 147456
  655.8 1.1 copy-start.2
  659.8 410.7 %reduce-scatter.9.cloned.1.call-start = ((), (), s32[]{:S(2)}) async-start(), calls=%async_computation.8 | async-start | bytes 294912 | tf_op jit(solution)/shard_map/reduce_scatter | solution.py:55
  664.2 503.1 %reduce-scatter.11.cloned.1.call-start = ((), (), s32[]{:S(2)}) async-start(), calls=%async_computation.9 | async-start | bytes 2359296 | tf_op jit(solution)/shard_map/reduce_scatter | solution.py:61
Sparse Core Ops, SparseCore 0:
  9.9 67.1 all-gather.1
  82.1 280.0 all-reduce.3
  376.7 276.6 all-reduce.5
  656.4 137.5 reduce-scatter.6
  797.2 105.3 all-reduce.7
  906.2 80.9 reduce-scatter.12
  991.1 79.3 reduce-scatter.8
  1075.1 92.1 reduce-scatter.10
where the time goes:
time: 1180 us
  waiting for transfers between devices  1080 us (92%)
  matrix products  35.6 us (3%)
  blocking collectives  21.5 us (2%)
  between operations  14.3 us (1%)
  other arithmetic  12.4 us (1%)
    psum x1, waiting for transfers between devices, body(): lax.psum(jnp.dot(hidden, second_weight, preferred_element_type=jnp.float3...  277 us
    psum x1, waiting for transfers between devices, body(): lax.psum(feat_grad_part.astype(jnp.bfloat16), 'center').astype(jnp.float32)  269 us
    reduce_scatter x1, waiting for transfers between devices, body(): lax.psum_scatter(pred_part.astype(jnp.bfloat16), 'center', scatter_dimens...  123 us
    psum x1, waiting for transfers between devices, body(): lax.psum(coef_grad.astype(jnp.bfloat16), 'dp').astype(jnp.float32)  107 us
    reduce_scatter x1, waiting for transfers between devices, body(): lax.psum_scatter(center_grad.astype(jnp.bfloat16), 'dp', scatter_dimensio...  95.4 us
    reduce_scatter x1, waiting for transfers between devices, body(): lax.psum_scatter(first_grad.astype(jnp.bfloat16), 'dp', scatter_dimension...  81.8 us
    all_gather x1, waiting for transfers between devices, body(): gathered = lax.all_gather(embeddings, 'center', axis=1, tiled=True)  69.1 us
    unnamed x9, waiting for transfers between devices  61.5 us
  transfers between devices with their start and end apart: 8, of which 8 were waited for; matrix products, arithmetic and copies ran while one was open for 3% of the time, Pallas kernels for 0%

commit v1 on v0

v1 whole, which is shorter than its diff:
```python
import functools
import math

import jax
import jax.numpy as jnp
from jax import lax
from jax.experimental import pallas as pl
from jax.experimental.pallas import tpu as pltpu
from jax.sharding import PartitionSpec as P

MESH = pl.DeviceIdType.MESH
F32 = jnp.float32
BF16 = jnp.bfloat16
ORDER = (0, 1, 3, 2)
GELU_C = math.sqrt(2.0 / math.pi)
LOG2E = math.log2(math.e)
SEMS = 96


def dot(a, b):
    return jnp.dot(a, b, preferred_element_type=F32)


def kernel(emb, w1, b1, w2, ctr, coef, cot,
           o_pred, o_first, o_second, o_bias, o_cg, o_coef,
           emb_sib, emb_pair, w_sib, w_pair, b_mine, b_sib, b_pair, wg, sg, bg, g, gt,
           pre, hid, gd, part, part_in, zs, zown, zr, sq, f, ft, ct, qp, qt, cn, cotp, cott,
           fg, pr, rs, cg, cf, cs, rp, prv, xown, xs_out, xr, z2, z2own, z2r, ph,
           cgs, cgr, cgh, cghr, cfs, cfr, cfh, cfhr, tt, tr, u, v, hs, hb, tot,
           ssem, rsem):
    dp = lax.axis_index("dp")
    c = lax.axis_index("center")
    y, h = dp // 2, dp % 2
    zl, x, k = c // 8, (c // 2) % 4, c % 2
    feat = 512
    factor = 16.0 / feat
    scale = 8.0 / feat * LOG2E

    def dev(xx=None, yy=None, hh=None, zz=None, kk=None):
        xx = x if xx is None else xx
        yy = y if yy is None else yy
        hh = h if hh is None else hh
        zz = zl if zz is None else zz
        kk = k if kk is None else kk
        return {"dp": yy * 2 + hh, "center": zz * 8 + xx * 2 + kk}

    def plus(a, d):
        return lax.rem(a + d, 4)

    def minus(a, d):
        return lax.rem(a + 4 - d, 4)

    ids = {"s": 0, "r": 0}
    sent = []

    def new(kind, n=1):
        first = ids[kind]
        ids[kind] += n
        assert ids[kind] <= SEMS
        return first

    def remote(src, dst, target, sid, rid):
        return pltpu.make_async_remote_copy(
            src_ref=src, dst_ref=dst, send_sem=ssem.at[sid], recv_sem=rsem.at[rid],
            device_id=target, device_id_type=MESH)

    def send(src, dst, target, rid=None):
        rid = new("r") if rid is None else rid
        cp = remote(src, dst, target, new("s"), rid)
        cp.start()
        sent.append(cp)
        return cp

    def to_home(src, dst_at, rid_at):
        rid = rid_at
        for d in (1, 3, 2):
            send(src, dst_at, dev(xx=plus(x, d), kk=x // 2), rid)
        sid = new("s")

        @pl.when(k == x // 2)
        def _():
            pltpu.make_async_copy(src, dst_at, rsem.at[rid]).start()

        @pl.when(k != x // 2)
        def _():
            remote(src, dst_at, dev(kk=1 - k), sid, rid).start()
        homes.append((src, dst_at, sid))

    homes = []

    barrier = pltpu.get_barrier_semaphore()
    peers = [dev(kk=1 - k), dev(hh=1 - h)]
    for d in (1, 2, 3):
        peers += [dev(xx=plus(x, d)), dev(xx=plus(x, d), kk=1 - k), dev(zz=plus(zl, d)), dev(yy=plus(y, d))]
    for peer in peers:
        pl.semaphore_signal(barrier, inc=1, device_id=peer, device_id_type=MESH)
    b_mine[...] = jnp.broadcast_to(b1[...], b_mine.shape)
    pl.semaphore_wait(barrier, len(peers))
    sib = dev(kk=1 - k)

    c_emb = send(emb.at[:, :, 1 - k], emb_sib, sib)
    c_w = send(w1.at[1 - k], w_sib, sib)
    c_b = send(b_mine, b_sib, sib)

    r_sg = new("r", 4)
    to_home(w2, sg.at[x % 2, k], r_sg + 2 * (x % 2) + k)

    def paired(mine, other):
        low = jnp.where(k == 0, mine, other)
        high = jnp.where(k == 0, other, mine)
        return jnp.concatenate([low, high], axis=-1)

    c_emb.wait_recv()
    for xx in range(4):
        emb_pair[xx] = paired(emb[:, xx, k].reshape(128, 64), emb_sib[:, xx].reshape(128, 64))
    c_x = {}
    for d in (1, 3, 2):
        c_x[d] = send(emb_pair.at[plus(x, d)], g.at[zl, x, k], dev(xx=plus(x, d)))
    g[zl, x, k] = emb_pair[x]

    c_w.wait_recv()
    w_pair[...] = paired(w1[k], w_sib[...]).reshape(2, 512, 128)
    r_w = new("r", 4)
    to_home(w_pair, wg.at[x % 2, pl.ds(2 * k, 2)], r_w + 2 * (x % 2) + k)
    c_b.wait_recv()
    b_pair[...] = paired(b_mine[:, :64], b_sib[:, :64])
    r_b = new("r", 4)
    to_home(b_pair, bg.at[x % 2, k], r_b + 2 * (x % 2) + k)

    c_z = {}
    for d in ORDER:
        xx = minus(x, d)
        if d:
            c_x[d].wait_recv()
        piece = g.at[zl, xx, k]
        for e in (1, 3, 2):
            c_z[d, e] = send(piece, piece, dev(zz=plus(zl, e)))
    c_gs = {0: send(g.at[zl, :, k], g.at[zl, :, k], sib)}

    qp[...] = jnp.zeros_like(qp)
    cotp[...] = jnp.zeros_like(cotp)
    for xx in range(4):
        for kk in range(2):
            for zz in range(4):
                cotp[xx, pl.ds((kk * 4 + zz) * 32, 32), :100] = cot[zz, xx, kk]

    def prepare(t, carry):
        qp[t, :, :100] = coef[t]
        qt[t] = qp[t].T
        turned = ctr[t].T
        ct[t] = turned
        wide = turned.astype(F32)
        cn[t] = jnp.broadcast_to(jnp.sum(wide * wide, axis=0, keepdims=True) * scale, (8, 512))
        cott[t] = cotp[t].T
        cg[t] = jnp.zeros((512, 512), F32)
        cf[t] = jnp.zeros((128, 512), F32)
        cs[t] = jnp.zeros((8, 512), F32)
        return carry

    lax.fori_loop(0, 4, prepare, 0)

    def wait_home(ref, first):
        for i in range(2):
            for j in range(2):
                pltpu.make_async_copy(ref.at[i, pl.ds(2 * j, 2)] if ref is wg else ref.at[i, j],
                                      ref.at[i, pl.ds(2 * j, 2)] if ref is wg else ref.at[i, j],
                                      rsem.at[first + 2 * i + j]).wait()

    wait_home(sg, r_sg)
    wait_home(wg, r_w)
    wait_home(bg, r_b)

    acc = jnp.zeros((256, 256), F32)
    for e in ORDER:
        src = minus(zl, e)
        if e:
            for d in ORDER:
                c_z[d, e].wait_recv()
            c_gs[e] = send(g.at[src, :, k], g.at[src, :, k], sib)
        c_gs[e].wait_recv()
        lhs = jnp.concatenate([g[src, xx].reshape(256, 128) for xx in range(4)], axis=1)
        rhs = jnp.concatenate([wg[0, src], wg[1, src]], axis=1)
        acc = acc + dot(lhs, rhs)
    bias = jnp.concatenate([bg[0, 0], bg[1, 0]], axis=1)[0:1]
    pre[...] = acc + bias
    u0 = pre[...]
    t0 = jnp.tanh(GELU_C * (u0 + 0.044715 * (u0 * u0 * u0)))
    hid[...] = (u0 * (0.5 * (1.0 + t0))).astype(BF16)
    second = sg[...].reshape(256, 512)
    part[...] = dot(hid[...], second).reshape(2, 128, 512)
    c_p = send(part.at[1 - k], part_in, sib)
    gd[...] = 0.5 * (1.0 + t0) + 0.5 * u0 * (1.0 - t0 * t0) * (GELU_C * (1.0 + 3.0 * 0.044715 * (u0 * u0)))
    c_p.wait_recv()
    summed = (part[k] + part_in[...]).reshape(4, 32, 512)
    zown[...] = summed
    zs[...] = summed.astype(BF16)
    c_f = {}
    for e in (1, 3, 2):
        c_f[e] = send(zs.at[plus(zl, e)], zr.at[e - 1], dev(zz=plus(zl, e)))
    for zz in range(4):
        for xx in range(4):
            gt[zz * 2 + xx // 2, pl.ds((xx % 2) * 128, 128)] = g[zz, xx].reshape(256, 128).T
    total = zown[zl]
    for e in (1, 3, 2):
        c_f[e].wait_recv()
        total = total + zr[e - 1].astype(F32)
    squashed = jnp.tanh(total)
    sq[...] = squashed
    f[x, k, zl] = squashed.astype(BF16)

    c_fz = [send(f.at[x, k, zl], f.at[x, k, zl], dev(zz=plus(zl, e))) for e in (1, 3, 2)]
    for cp in c_fz:
        cp.wait_recv()
    c_fs = {0: send(f.at[x, k], f.at[x, k], sib)}
    c_fx = {d: send(f.at[x, k], f.at[x, k], dev(xx=plus(x, d))) for d in (1, 3, 2)}

    c_pair = {}
    c_xr = {}

    def finish_pair(i):
        c_pair[i].wait_recv()
        both = rp[i, k].astype(F32) + prv[i].astype(F32)
        if i == 0:
            xown[...] = both
        else:
            xs_out[i - 1] = both.astype(BF16)
            c_xr[i] = send(xs_out.at[i - 1], xr.at[i - 1], dev(xx=minus(x, ORDER[i])))

    for i, d in enumerate(ORDER):
        xx = minus(x, d)
        c_fs[d].wait_recv()
        fx = f[xx].reshape(256, 512)
        wide = fx.astype(F32)
        fn = jnp.sum(wide * wide, axis=1, keepdims=True) * scale
        ft[...] = fx.T
        fg[...] = jnp.zeros_like(fg)
        pr[...] = jnp.zeros_like(pr)
        rs[...] = jnp.zeros_like(rs)

        def tile(t, carry):
            fx = f[xx].reshape(256, 512)
            inner = dot(fx, ct[t])
            low = jnp.exp2((2.0 * scale) * inner - (fn + cn[t, 0:1])).astype(BF16)
            weighted = dot(cotp[xx], qt[t]) * low.astype(F32)
            wlow = weighted.astype(BF16)
            rs[...] += (weighted[:, 0:128] + weighted[:, 128:256]) + (weighted[:, 256:384] + weighted[:, 384:512])
            cs[t] += jnp.sum(weighted.reshape(32, 8, 512), axis=0)
            pr[...] += dot(low, qp[t])
            fg[...] += dot(wlow, ctr[t])
            cg[t] += dot(ft[...], wlow)
            cf[t] += dot(cott[xx], low)
            return carry

        lax.fori_loop(0, 2, tile, 0)
        if i < 3:
            nxt = ORDER[i + 1]
            c_fx[nxt].wait_recv()
            c_fs[nxt] = send(f.at[minus(x, nxt), k], f.at[minus(x, nxt), k], sib)
        if i > 0:
            finish_pair(i - 1)
        lax.fori_loop(2, 4, tile, 0)
        fx = f[xx].reshape(256, 512)
        rows = jnp.sum(rs[...], axis=1, keepdims=True)
        fgrad = -factor * (rows * fx.astype(F32) - fg[...])
        rp[i, :, :, :512] = fgrad.astype(BF16).reshape(2, 128, 512)
        rp[i, :, :, 512:] = pr[...].astype(BF16).reshape(2, 128, 128)
        c_pair[i] = send(rp.at[i, 1 - k], prv.at[i], sib)

    def center_out(t, carry):
        column = jnp.sum(cs[t], axis=0, keepdims=True)
        grad = -factor * (column * ct[t].astype(F32) - cg[t])
        cgs[:, t] = grad.astype(BF16).reshape(4, 128, 512)
        cfs[t] = cf[t, 0:112].astype(BF16)
        return carry

    lax.fori_loop(0, 4, center_out, 0)
    finish_pair(3)
    c_cg = {e: send(cgs.at[plus(y, e)], cgr.at[e - 1], dev(yy=plus(y, e))) for e in (1, 3, 2)}
    r_cf = new("r", 4)
    for e in (1, 3, 2):
        send(cfs.at[plus(y, e)], cfr.at[y], dev(yy=plus(y, e)), r_cf + y)
    cfr[y] = cfs[y]

    total = xown[...]
    for i in (1, 2, 3):
        c_xr[i].wait_recv()
        total = total + xr[i - 1].astype(F32)
    total = total.reshape(4, 32, 640)
    z2own[...] = total
    z2[...] = total.astype(BF16)
    c_z2 = {e: send(z2.at[plus(zl, e)], z2r.at[e - 1], dev(zz=plus(zl, e))) for e in (1, 3, 2)}
    total = z2own[zl]
    for e in (1, 3, 2):
        c_z2[e].wait_recv()
        total = total + z2r[e - 1].astype(F32)
    o_pred[...] = total[:, 512:612]
    phi = (total[:, :512] * (1.0 - sq[...] * sq[...])).astype(BF16)
    ph[k, zl] = phi
    c_ph = [send(ph.at[k, zl], ph.at[k, zl], dev(zz=plus(zl, e))) for e in (1, 3, 2)]
    for cp in c_ph:
        cp.wait_recv()
    c_phs = send(ph.at[k], ph.at[k], sib)
    c_phs.wait_recv()

    phi_all = ph[...].reshape(256, 512)
    hgrad = lax.dot_general(phi_all, sg[...].reshape(256, 512), (((1,), (1,)), ((), ())), preferred_element_type=F32)
    pgrad = hgrad * gd[...]
    bias_grad = jnp.sum(pgrad, axis=0, keepdims=True)
    plow = pgrad.astype(BF16)
    phit = phi_all.T
    bias_rows = jnp.broadcast_to(bias_grad, (16, 256)).astype(BF16)
    second_grad = dot(phit, hid[...]).astype(BF16)
    for yy in range(4):
        for hh in range(2):
            q = 2 * yy + hh
            tt[yy, hh, 0:256] = dot(gt[q], plow).astype(BF16)
            tt[yy, hh, 256:320] = second_grad[64 * q:64 * q + 64]
            tt[yy, hh, 320:336] = bias_rows
    r_t = new("r", 4)
    for e in (2, 1, 3):
        send(tt.at[plus(y, e)], tr.at[y], dev(yy=plus(y, e)), r_t + y)
    tr[y] = tt[y]

    for e in (1, 3, 2):
        c_cg[e].wait_recv()

    def center_sum(t, carry):
        s = cgs[y, t].astype(F32)
        for e in (1, 3, 2):
            s = s + cgr[e - 1, t].astype(F32)
        s = s.reshape(2, 64, 512)
        cgh[t] = s.astype(BF16)
        o_cg[t] = jnp.where(h == 0, s[0], s[1])
        return carry

    lax.fori_loop(0, 4, center_sum, 0)
    c_ch = send(cgh.at[:, 1 - h], cghr, dev(hh=1 - h))

    def wait_slots(ref, first, own):
        for j in range(4):
            @pl.when(own != j)
            def _():
                pltpu.make_async_copy(ref.at[j], ref.at[j], rsem.at[first + j]).wait()

    wait_slots(cfr, r_cf, y)
    s = (cfr[0].astype(F32) + cfr[1].astype(F32)) + (cfr[2].astype(F32) + cfr[3].astype(F32))
    cfh[...] = s.astype(BF16)
    c_cfh = send(cfh, cfhr, dev(hh=1 - h))

    wait_slots(tr, r_t, y)
    for hh in range(2):
        s = (tr[0, hh].astype(F32) + tr[1, hh].astype(F32)) + (tr[2, hh].astype(F32) + tr[3, hh].astype(F32))
        low = s.astype(BF16)
        u[0, hh] = low[:, :128]
        u[1, hh] = low[:, 128:]
    r_v = new("r", 4)
    x_sends = []
    for j in range(2):
        for hh in range(2):
            sid = new("s")
            mine = jnp.logical_and(x == 2 * k + j, k == hh)
            src, dst, rid = u.at[j, hh], v.at[x], r_v + x
            x_sends.append((src, dst, sid, mine))

            @pl.when(mine)
            def _():
                pltpu.make_async_copy(src, dst, rsem.at[rid]).start()

            @pl.when(jnp.logical_not(mine))
            def _():
                remote(src, dst, dev(xx=2 * k + j, kk=hh), sid, rid).start()

    c_cfh.wait_recv()
    o_coef[y] = (cfh[...].astype(F32) + cfhr[...].astype(F32)).astype(BF16)
    r_o = new("r", 4)
    for e in (1, 3, 2):
        send(o_coef.at[y], o_coef.at[y], dev(yy=plus(y, e)), r_o + y)

    for j in range(4):
        pltpu.make_async_copy(v.at[j], v.at[j], rsem.at[r_v + j]).wait()
    s = (v[0].astype(F32) + v[1].astype(F32)) + (v[2].astype(F32) + v[3].astype(F32))
    hs[...] = s.astype(BF16)
    s_across, r_across, s_last, r_last = new("s"), new("r"), new("s"), new("r")

    @pl.when(k != h)
    def _():
        remote(hs, hb, dev(hh=1 - h, kk=k), s_across, r_across).start()

    c_ch.wait_recv()
    o_cg[...] += cghr[...].astype(F32)

    @pl.when(k == h)
    def _():
        pltpu.make_async_copy(hb, hb, rsem.at[r_across]).wait()
        tot[...] = hs[...].astype(F32) + hb[...].astype(F32)
        remote(tot, tot, sib, s_last, r_last).start()

    @pl.when(k != h)
    def _():
        pltpu.make_async_copy(tot, tot, rsem.at[r_last]).wait()

    whole = tot[...]
    half = jnp.where(k == 0, whole[:, :64], whole[:, 64:])
    o_first[...] = half[0:256]
    o_second[...] = half[256:320]
    o_bias[...] = half[320:328]
    wait_slots(o_coef, r_o, y)

    for cp in sent:
        cp.wait_send()
    for src, dst, sid in homes:
        @pl.when(k != x // 2)
        def _():
            pltpu.make_async_copy(src, src, ssem.at[sid]).wait()
    for src, dst, sid, mine in x_sends:
        @pl.when(jnp.logical_not(mine))
        def _():
            pltpu.make_async_copy(src, src, ssem.at[sid]).wait()

    @pl.when(k != h)
    def _():
        pltpu.make_async_copy(hs, hs, ssem.at[s_across]).wait()

    @pl.when(k == h)
    def _():
        pltpu.make_async_copy(tot, tot, ssem.at[s_last]).wait()


SCRATCH = (
    ("emb_sib", (4, 4, 32, 64), BF16), ("emb_pair", (4, 128, 128), BF16), ("w_sib", (1024, 64), BF16),
    ("w_pair", (2, 512, 128), BF16), ("b_mine", (8, 128), F32), ("b_sib", (8, 128), F32), ("b_pair", (8, 128), F32),
    ("wg", (2, 4, 512, 128), BF16), ("sg", (2, 2, 64, 512), BF16), ("bg", (2, 2, 8, 128), F32),
    ("g", (4, 4, 2, 128, 128), BF16), ("gt", (8, 256, 256), BF16),
    ("pre", (256, 256), F32), ("hid", (256, 256), BF16), ("gd", (256, 256), F32),
    ("part", (2, 128, 512), F32), ("part_in", (128, 512), F32),
    ("zs", (4, 32, 512), BF16), ("zown", (4, 32, 512), F32), ("zr", (3, 32, 512), BF16), ("sq", (32, 512), F32),
    ("f", (4, 2, 4, 32, 512), BF16), ("ft", (512, 256), BF16), ("ct", (4, 512, 512), BF16),
    ("qp", (4, 512, 128), BF16), ("qt", (4, 128, 512), BF16), ("cn", (4, 8, 512), F32),
    ("cotp", (4, 256, 128), BF16), ("cott", (4, 128, 256), BF16),
    ("fg", (256, 512), F32), ("pr", (256, 128), F32), ("rs", (256, 128), F32),
    ("cg", (4, 512, 512), F32), ("cf", (4, 128, 512), F32), ("cs", (4, 8, 512), F32),
    ("rp", (4, 2, 128, 640), BF16), ("prv", (4, 128, 640), BF16), ("xown", (128, 640), F32),
    ("xs_out", (3, 128, 640), BF16), ("xr", (3, 128, 640), BF16),
    ("z2", (4, 32, 640), BF16), ("z2own", (4, 32, 640), F32), ("z2r", (3, 32, 640), BF16), ("ph", (2, 4, 32, 512), BF16),
    ("cgs", (4, 4, 128, 512), BF16), ("cgr", (3, 4, 128, 512), BF16), ("cgh", (4, 2, 64, 512), BF16), ("cghr", (4, 64, 512), BF16),
    ("cfs", (4, 112, 512), BF16), ("cfr", (4, 112, 512), BF16), ("cfh", (112, 512), BF16), ("cfhr", (112, 512), BF16),
    ("tt", (4, 2, 336, 256), BF16), ("tr", (4, 2, 336, 256), BF16), ("u", (2, 2, 336, 128), BF16),
    ("v", (4, 336, 128), BF16), ("hs", (336, 128), BF16), ("hb", (336, 128), BF16), ("tot", (336, 128), F32),
)


def body(embeddings, first_weight, first_bias, second_weight, centers, coefficients, cotangent):
    args = (
        embeddings.reshape(4, 4, 2, 32, 64),
        first_weight.reshape(2, 1024, 64),
        jnp.pad(first_bias.reshape(1, 64), ((0, 0), (0, 64))),
        second_weight,
        centers.reshape(4, 512, 512),
        coefficients.reshape(4, 512, 100),
        cotangent.reshape(4, 4, 2, 32, 100),
    )
    vmem = pl.BlockSpec(memory_space=pltpu.VMEM)
    outs = (
        jax.ShapeDtypeStruct((32, 100), F32),
        jax.ShapeDtypeStruct((256, 64), F32),
        jax.ShapeDtypeStruct((64, 64), F32),
        jax.ShapeDtypeStruct((8, 64), F32),
        jax.ShapeDtypeStruct((4, 64, 512), F32),
        jax.ShapeDtypeStruct((4, 112, 512), BF16),
    )
    predictions, grad_first, grad_second, grad_bias, grad_centers, grad_coefs = pl.pallas_call(
        kernel,
        out_shape=outs,
        in_specs=[vmem] * len(args),
        out_specs=[vmem] * len(outs),
        scratch_shapes=[pltpu.VMEM(shape, dtype) for name, shape, dtype in SCRATCH]
        + [pltpu.SemaphoreType.DMA((SEMS,)), pltpu.SemaphoreType.DMA((SEMS,))],
        compiler_params=pltpu.CompilerParams(collective_id=0, has_side_effects=True, vmem_limit_bytes=60 << 20),
        name="layer",
    )(*args)
    return (
        predictions,
        grad_first,
        grad_bias[0],
        grad_second.T,
        grad_centers.transpose(0, 2, 1).reshape(2048, 64),
        grad_coefs.transpose(0, 2, 1)[:, :, :100].reshape(2048, 100).astype(F32),
    )


def solution(mesh):
    placed = (
        P("dp", "center"),
        P(None, "center"),
        P("center"),
        P("center", None),
        P("center", None),
        P("center", None),
        P("dp", None),
    )
    return jax.shard_map(
        body,
        mesh=mesh,
        in_specs=placed,
        out_specs=(
            P(("dp", "center"), None),
            P("dp", "center"),
            P("center"),
            P("center", "dp"),
            P("center", "dp"),
            P("center", None),
        ),
        check_vma=False,
    )
```

time: 1180 us -> 143 us (0.12)
  waiting for transfers between devices: 1080 us -> 0 us
  Pallas kernels: 0 us -> 123 us
  matrix products: 35.6 us -> 0 us
  blocking collectives: 21.5 us -> 0 us
  between operations: 14.3 us -> 0.68 us
    psum x3 -> x0, waiting for transfers between devices: 653 us -> none  [the longest x1 277 us: body(): lax.psum(jnp.dot(hidden, second_weight, preferred_element_type=jnp.float3...]
    reduce_scatter x3 -> x0, waiting for transfers between devices: 300 us -> none  [the longest x1 123 us: body(): lax.psum_scatter(pred_part.astype(jnp.bfloat16), 'center', scatter_dimens...]
    pallas_call x0 -> x1, Pallas kernels: none -> 123 us  [body(): pl.pallas_call(kernel, out_shape=outs, in_specs=[vmem] * len(args), out_s...]
    all_gather x1 -> x0, waiting for transfers between devices: 69.1 us -> none  [body(): gathered = lax.all_gather(embeddings, 'center', axis=1, tiled=True)]
    unnamed x9 -> x0, waiting for transfers between devices: 61.5 us -> none
    dot_general x11 -> x0, matrix products: 35.6 us -> none  [the longest x1 6.53 us: body(): jnp.einsum('tc,tf->cf', weighted_low, features, preferred_element_type=jn...]
    psum x1 -> x0, blocking collectives: 21.5 us -> none  [body(): lax.psum(bias_grad.astype(jnp.bfloat16), 'dp').astype(jnp.float32)]
  transfers between devices with their start and end apart: 8 -> 0, of which waited for: 8 -> 0; matrix products, arithmetic and copies ran while one was open for 3% -> 0% of each run, Pallas kernels for 0% -> 0%
where the time goes in v1:
time: 143 us; the launch traced here: 142 us
  Pallas kernels  123 us (86%)
  local copies, waits for them, and re-layouts  17.3 us (12%)
    pallas_call x1, Pallas kernels, body(): pl.pallas_call(kernel, out_shape=outs, in_specs=[vmem] * len(args), out_s...  123 us
    unnamed x11, local copies, waits for them, and re-layouts  12.5 us

profile of v1, /device:TPU:1, one launch (start us, length us, event | category | flops | bytes accessed | tf_op | source)
XLA Modules:
  0.0 142.3 jit_solution(13549761333516783307)
XLA Ops:
  0.6 1.2 pad.4.b1
  1.8 1.8 %copy.19 = bf16[1024,64]{1,0:T(8,128)(2,1)} copy(bf16[1024,64]{0,1:T(8,128)(2,1)} %param.7) | data formatting | bytes 262144 | tf_op args[0]
  3.6 1.8 %copy.22 = bf16[1024,100]{1,0:T(8,128)(2,1)} copy(bf16[1024,100]{0,1:T(8,128)(2,1)} %param.13) | data formatting | bytes 409600 | tf_op args[6]
  5.4 2.0 %copy.20 = bf16[2048,64]{1,0:T(8,128)(2,1)} copy(bf16[2048,64]{0,1:T(8,128)(2,1)} %param.8) | data formatting | bytes 524288 | tf_op args[1]
  7.3 2.0 %copy.21 = bf16[2048,100]{1,0:T(8,128)(2,1)} copy(bf16[2048,100]{0,1:T(8,128)(2,1)} %param.12) | data formatting | bytes 819200 | tf_op args[5]
  9.3 123.2 %layer.1 = (f32[32,100]{1,0:T(8,128)}, f32[256,64]{1,0:T(8,128)}, f32[64,64]{1,0:T(8,128)}, f32[8,64]{1,0:T(8,128)}, f32[4,64,512]{2,1,0:T(8,128)}, /*index=5*/bf16[4,112,512]{2,1,0:T(8,128)(2,1)}) custom-call(bf16[4,4,2,32,64]{4,3,2,1,0:T(8,128)(2,1)} %bitcast.25, bf16[2,1024,64]{2,1,0:T(8,128)(2,1)} %bitcast.23, f32[1,128]{1,0:T(1,128)} %pad.4.b1, ...), custom_call_target="tpu_custom_call" | custom-call | tf_op jit(solution)/shard_map/layer/pallas_call | solution.py:471
  132.6 1.2 slice_bitcast_fusion
  133.8 1.5 %copy.26 = f32[64,64]{1,0:T(8,128)} copy(f32[64,64]{0,1:T(8,128)} %bitcast.31) | data formatting | bytes 32768
  135.2 1.6 %copy.25 = f32[256,64]{0,1:T(8,128)} copy(f32[256,64]{1,0:T(8,128)} %get-tuple-element.25) | data formatting | bytes 131072
  136.8 1.9 %copy.27 = f32[4,8,8,512]{3,2,0,1:T(8,128)} copy(f32[4,8,8,512]{3,2,1,0:T(8,128)} %bitcast.29) | data formatting | bytes 1048576 | tf_op jit(solution)/shard_map/reshape | solution.py:486
  138.7 1.1 slice_convert_fusion
  139.8 0.5 copy.30
  140.3 0.0 copy-start
  140.4 0.1 pad.5
  140.5 1.2 copy.28
  141.7 0.0 copy-done
  141.7 0.6 copy.32
Async XLA Ops:
  140.3 1.3 copy-start

commit v2 on v1

v2 whole, which is shorter than its diff:
```python
import functools
import math

import jax
import jax.numpy as jnp
from jax import lax
from jax.experimental import pallas as pl
from jax.experimental.pallas import tpu as pltpu
from jax.sharding import PartitionSpec as P

MESH = pl.DeviceIdType.MESH
F32 = jnp.float32
BF16 = jnp.bfloat16
ORDER = (0, 1, 3, 2)
GELU_C = math.sqrt(2.0 / math.pi)
LOG2E = math.log2(math.e)
SEMS = 160


def dot(a, b):
    return jnp.dot(a, b, preferred_element_type=F32)


def kernel(embt_hbm, w1t_hbm, b1, w2, ctr_hbm, coeft_hbm, cott_hbm,
           o_pred, o_first, o_second, o_bias, o_cg, o_coef,
           embt, w1t, ctr, coeft, cott_in, emb_sib, emb_all, w_sib, w_pair, b_mine, b_sib, b_pair, wg, sg, bg, g, gt,
           hid, gd, part, part_in, zs, zown, zr, sq, f, ft, ct,
           qp, qt, cn, cot_pad, cot_all, cotp, cott, kg, kb, wb,
           rs, cs, rp, prv, xown, xs_out, xr, z2, z2own, z2r, ph,
           cgs, cgr, cgh, cghr, cfs, cfr, cfh, cfhr, tt, tr, u, v, tb, vb, ub, yb, mix, hs, ha, hb,
           ssem, rsem):
    dp = lax.axis_index("dp")
    c = lax.axis_index("center")
    y, h = dp // 2, dp % 2
    zl, x, k = c // 8, (c // 2) % 4, c % 2
    feat = 512
    factor = 16.0 / feat
    scale = 8.0 / feat * LOG2E

    def dev(xx=None, yy=None, hh=None, zz=None, kk=None):
        xx = x if xx is None else xx
        yy = y if yy is None else yy
        hh = h if hh is None else hh
        zz = zl if zz is None else zz
        kk = k if kk is None else kk
        return {"dp": yy * 2 + hh, "center": zz * 8 + xx * 2 + kk}

    def plus(a, d):
        return lax.rem(a + d, 4)

    def minus(a, d):
        return lax.rem(a + 4 - d, 4)

    ids = {"s": 0, "r": 0}
    sent = []

    def new(kind, n=1):
        first = ids[kind]
        ids[kind] += n
        assert ids[kind] <= SEMS
        return first

    def remote(src, dst, target, sid, rid):
        return pltpu.make_async_remote_copy(
            src_ref=src, dst_ref=dst, send_sem=ssem.at[sid], recv_sem=rsem.at[rid],
            device_id=target, device_id_type=MESH)

    def send(src, dst, target, rid=None):
        rid = new("r") if rid is None else rid
        cp = remote(src, dst, target, new("s"), rid)
        cp.start()
        sent.append(cp)
        return cp

    def to_home(src, dst_at, rid_at):
        rid = rid_at
        for d in (1, 3, 2):
            send(src, dst_at, dev(xx=plus(x, d), kk=x // 2), rid)
        sid = new("s")

        @pl.when(k == x // 2)
        def _():
            pltpu.make_async_copy(src, dst_at, rsem.at[rid]).start()

        @pl.when(k != x // 2)
        def _():
            remote(src, dst_at, dev(kk=1 - k), sid, rid).start()
        homes.append((src, dst_at, sid))

    homes = []

    barrier = pltpu.get_barrier_semaphore()
    peers = [dev(kk=1 - k), dev(hh=1 - h), dev(hh=1 - h, kk=1 - k)]
    for d in (1, 2, 3):
        peers += [dev(xx=plus(x, d)), dev(xx=plus(x, d), kk=1 - k), dev(zz=plus(zl, d)), dev(yy=plus(y, d))]
    for peer in peers:
        pl.semaphore_signal(barrier, inc=1, device_id=peer, device_id_type=MESH)
    loads = []
    own_half = pl.ds(pl.multiple_of(k * 1024, 1024), 1024)
    for src, dst in ((embt_hbm, embt), (w1t_hbm.at[:, own_half], w1t), (cott_hbm, cott_in), (coeft_hbm, coeft), (ctr_hbm, ctr)):
        loads.append(pltpu.make_async_copy(src, dst, rsem.at[new("r")]))
        loads[-1].start()
    wide_bias = jnp.broadcast_to(b1[...], (8, 64))
    b_mine[...] = jnp.concatenate([wide_bias, wide_bias], axis=1)
    pl.semaphore_wait(barrier, len(peers))
    sib = dev(kk=1 - k)

    c_emb = send(embt_hbm, emb_sib, sib)
    c_w = send(w1t_hbm.at[:, pl.ds(pl.multiple_of((1 - k) * 1024, 1024), 1024)], w_sib, sib)
    c_b = send(b_mine, b_sib, sib)

    def paired(mine, other):
        low = jnp.where(k == 0, mine, other)
        high = jnp.where(k == 0, other, mine)
        return jnp.concatenate([low, high], axis=0)

    loads[0].wait()
    c_emb.wait_recv()
    emb_all[...] = paired(embt[...], emb_sib[...]).T.reshape(4, 4, 2, 32, 128)
    c_x = {}
    for d in (1, 3, 2):
        c_x[d] = send(emb_all.at[:, plus(x, d), k], g.at[zl, x, k], dev(xx=plus(x, d)))
    g[zl, x, k] = emb_all[:, x, k]

    loads[1].wait()
    c_w.wait_recv()
    w_pair[...] = paired(w1t[...], w_sib[...]).T.reshape(2, 512, 128)
    r_w = new("r", 4)
    to_home(w_pair, wg.at[x % 2, pl.ds(2 * k, 2)], r_w + 2 * (x % 2) + k)
    c_b.wait_recv()
    lane = lax.broadcasted_iota(jnp.int32, (8, 128), 1)
    b_pair[...] = jnp.where((lane < 64) == (k == 0), b_mine[...], b_sib[...])
    r_b = new("r", 4)
    to_home(b_pair, bg.at[x % 2, k], r_b + 2 * (x % 2) + k)

    r_sg = new("r", 4)
    to_home(w2, sg.at[x % 2, k], r_sg + 2 * (x % 2) + k)

    c_z = {}
    for d in ORDER:
        xx = minus(x, d)
        if d:
            c_x[d].wait_recv()
        piece = g.at[zl, xx, k]
        for e in (1, 3, 2):
            c_z[d, e] = send(piece, piece, dev(zz=plus(zl, e)))
    c_gs = {0: send(g.at[zl, :, k], g.at[zl, :, k], sib)}

    for load in loads[2:]:
        load.wait()
    cot_pad[...] = jnp.zeros_like(cot_pad)
    cot_pad[0:100] = cott_in[...]
    cot_all[...] = cot_pad[...].T.reshape(4, 4, 2, 32, 128)
    for xx in range(4):
        for kk in range(2):
            cotp[xx, kk * 128:kk * 128 + 128] = cot_all[:, xx, kk].reshape(128, 128)
        cott[xx] = cotp[xx].T
    qt[...] = jnp.zeros_like(qt)
    for t in range(4):
        qt[t, 0:100] = coeft[:, t * 512:t * 512 + 512]

    def prepare(t, carry):
        rows = pl.ds(pl.multiple_of(t * 512, 512), 512)
        qp[rows] = qt[t].T
        turned = ctr[rows].T
        ct[t] = turned
        wide = turned.astype(F32)
        cn[t] = jnp.broadcast_to(jnp.sum(wide * wide, axis=0, keepdims=True) * scale, (8, 512))
        cs[t] = jnp.zeros((8, 512), F32)
        rs[t] = jnp.zeros((256, 128), F32)
        for xx in range(4):
            kg[xx, t] = dot(cotp[xx], qt[t])
        return carry

    lax.fori_loop(0, 4, prepare, 0)

    def wait_home(ref, first):
        for i in range(2):
            for j in range(2):
                pltpu.make_async_copy(ref.at[i, pl.ds(2 * j, 2)] if ref is wg else ref.at[i, j],
                                      ref.at[i, pl.ds(2 * j, 2)] if ref is wg else ref.at[i, j],
                                      rsem.at[first + 2 * i + j]).wait()

    wait_home(wg, r_w)

    acc = jnp.zeros((256, 256), F32)
    for n, e in enumerate(ORDER):
        src = minus(zl, e)
        if n < 3:
            nxt = ORDER[n + 1]
            for d in ORDER:
                c_z[d, nxt].wait_recv()
            c_gs[nxt] = send(g.at[minus(zl, nxt), :, k], g.at[minus(zl, nxt), :, k], sib)
        c_gs[e].wait_recv()
        lhs = jnp.concatenate([g[src, xx].reshape(256, 128) for xx in range(4)], axis=1)
        rhs = jnp.concatenate([wg[0, src], wg[1, src]], axis=1)
        acc = acc + dot(lhs, rhs)
    wait_home(bg, r_b)
    wait_home(sg, r_sg)
    bias = jnp.concatenate([bg[0, 0], bg[1, 0]], axis=1)[0:1]
    u0 = acc + bias
    t0 = jnp.tanh(GELU_C * (u0 + 0.044715 * (u0 * u0 * u0)))
    hid[...] = (u0 * (0.5 * (1.0 + t0))).astype(BF16)
    second = sg[...].reshape(256, 512)
    part[...] = dot(hid[...], second).reshape(2, 128, 512)
    c_p = send(part.at[1 - k], part_in, sib)
    gd[...] = 0.5 * (1.0 + t0) + 0.5 * u0 * (1.0 - t0 * t0) * (GELU_C * (1.0 + 3.0 * 0.044715 * (u0 * u0)))
    c_p.wait_recv()
    summed = (part[k] + part_in[...]).reshape(4, 32, 512)
    zown[...] = summed
    zs[...] = summed.astype(BF16)
    c_f = {}
    for e in (1, 3, 2):
        c_f[e] = send(zs.at[plus(zl, e)], zr.at[e - 1], dev(zz=plus(zl, e)))
    for zz in range(4):
        for xx in range(4):
            gt[zz * 2 + xx // 2, pl.ds((xx % 2) * 128, 128)] = g[zz, xx].reshape(256, 128).T
    total = zown[zl]
    for e in (1, 3, 2):
        c_f[e].wait_recv()
        total = total + zr[e - 1].astype(F32)
    squashed = jnp.tanh(total)
    sq[...] = squashed
    f[x, k, zl] = squashed.astype(BF16)

    own_piece = f.at[x, k, zl]
    c_fz = {e: send(own_piece, own_piece, dev(zz=plus(zl, e))) for e in (1, 3, 2)}
    c_fx = {}
    c_fp = {}
    for e in ORDER:
        if e:
            c_fz[e].wait_recv()
        piece = f.at[x, k, minus(zl, e)]
        c_fp[e] = send(piece, piece, sib)
        for d in (1, 3, 2):
            c_fx[d, e] = send(piece, piece, dev(xx=plus(x, d)))
    c_fs = {}

    def forward(d):
        for e in ORDER:
            c_fx[d, e].wait_recv()
        block = f.at[minus(x, d), k]
        c_fs[d] = send(block, block, sib)

    c_pair = {}
    c_xr = {}

    def finish_pair(i):
        c_pair[i].wait_recv()
        both = rp[i, k].astype(F32) + prv[i].astype(F32)
        if i == 0:
            xown[...] = both
        else:
            xs_out[i - 1] = both.astype(BF16)
            c_xr[i] = send(xs_out.at[i - 1], xr.at[i - 1], dev(xx=minus(x, ORDER[i])))

    def weigh(i, first, last):
        xx = minus(x, ORDER[i])
        here = slice(256 * i, 256 * i + 256)
        wide = f[xx].reshape(256, 512).astype(F32)
        fn = jnp.sum(wide * wide, axis=1, keepdims=True) * scale

        def tile(t, carry):
            inner = dot(f[xx].reshape(256, 512), ct[t])
            low = jnp.exp2((2.0 * scale) * inner - (fn + cn[t, 0:1])).astype(BF16)
            weighted = kg[xx, t] * low.astype(F32)
            kb[t, here] = low
            wb[t, here] = weighted.astype(BF16)
            rs[i] += (weighted[:, 0:128] + weighted[:, 128:256]) + (weighted[:, 256:384] + weighted[:, 384:512])
            cs[t] += jnp.sum(weighted.reshape(32, 8, 512), axis=0)
            return carry

        lax.fori_loop(first, last, tile, 0)

    c_cg = {}

    def center_out(t):
        column = jnp.sum(cs[t], axis=0, keepdims=True)
        grad = -factor * (column * ct[t].astype(F32) - dot(ft[...], wb[t]))
        cgs[:, t] = grad.astype(BF16).reshape(4, 128, 512)
        for e in (1, 3, 2):
            c_cg[t, e] = send(cgs.at[plus(y, e), t], cgr.at[e - 1, t], dev(yy=plus(y, e)))

    def wait_slots(ref, first, own):
        for j in range(4):
            @pl.when(own != j)
            def _():
                pltpu.make_async_copy(ref.at[j], ref.at[j], rsem.at[first + j]).wait()

    c_ch = {}

    def center_sum(t):
        s = cgs[y, t].astype(F32)
        for e in (1, 3, 2):
            c_cg[t, e].wait_recv()
            s = s + cgr[e - 1, t].astype(F32)
        s = s.reshape(2, 64, 512)
        cgh[t] = s.astype(BF16)
        o_cg[:, t * 512:t * 512 + 512] = jnp.where(h == 0, s[0], s[1])
        c_ch[t] = send(cgh.at[t, 1 - h], cghr.at[t], dev(hh=1 - h))

    def head_sums(i):
        xx = minus(x, ORDER[i])
        here = slice(256 * i, 256 * i + 256)
        low = jnp.concatenate([kb[t, here] for t in range(4)], axis=1)
        rp[i, :, :, 512:] = dot(low, qp[...]).astype(BF16).reshape(2, 128, 128)
        low = jnp.concatenate([wb[t, here] for t in range(4)], axis=1)
        rows = jnp.sum(rs[i], axis=1, keepdims=True)
        fgrad = -factor * (rows * f[xx].reshape(256, 512).astype(F32) - dot(low, ctr[...]))
        rp[i, :, :, :512] = fgrad.astype(BF16).reshape(2, 128, 512)
        c_pair[i] = send(rp.at[i, 1 - k], prv.at[i], sib)

    for e in ORDER:
        c_fp[e].wait_recv()
    for i, d in enumerate(ORDER):
        if i:
            c_fs[d].wait_recv()
        ft[:, 256 * i:256 * i + 256] = f[minus(x, d)].reshape(256, 512).T
        if i < 3:
            weigh(i, 0, 2)
            forward(ORDER[i + 1])
    weigh(3, 0, 1)
    center_out(0)
    weigh(3, 1, 2)
    center_out(1)
    for i in (1, 2, 3, 0):
        weigh(i, 2, 4)
        if i != 1:
            finish_pair((i + 3) % 4)
        head_sums(i)
    r_cf = new("r", 4)
    turned = jnp.concatenate([cott[minus(x, d)] for d in ORDER], axis=1)[0:112]
    for t in range(4):
        cfs[t] = dot(turned, kb[t]).astype(BF16)
    for e in (1, 3, 2):
        send(cfs.at[plus(y, e)], cfr.at[y], dev(yy=plus(y, e)), r_cf + y)
    cfr[y] = cfs[y]
    finish_pair(0)

    total = xown[...]
    for i in (1, 2, 3):
        c_xr[i].wait_recv()
        total = total + xr[i - 1].astype(F32)
    total = total.reshape(4, 32, 640)
    z2own[...] = total
    z2[...] = total.astype(BF16)
    c_z2 = {e: send(z2.at[plus(zl, e)], z2r.at[e - 1], dev(zz=plus(zl, e))) for e in (1, 3, 2)}
    center_out(2)
    center_out(3)
    center_sum(0)
    center_sum(1)
    total = z2own[zl]
    for e in (1, 3, 2):
        c_z2[e].wait_recv()
        total = total + z2r[e - 1].astype(F32)
    o_pred[...] = total[:, 512:612]
    phi = (total[:, :512] * (1.0 - sq[...] * sq[...])).astype(BF16)
    ph[k, zl] = phi
    c_ph = {e: send(ph.at[k, zl], ph.at[k, zl], dev(zz=plus(zl, e))) for e in (1, 3, 2)}
    wait_slots(cfr, r_cf, y)
    s = (cfr[0].astype(F32) + cfr[1].astype(F32)) + (cfr[2].astype(F32) + cfr[3].astype(F32))
    cfh[...] = s.astype(BF16)
    c_cfh = send(cfh, cfhr, dev(hh=1 - h))
    c_phs = []
    for e in ORDER:
        if e:
            c_ph[e].wait_recv()
        piece = ph.at[k, minus(zl, e)]
        c_phs.append(send(piece, piece, sib))
    for cp in c_phs:
        cp.wait_recv()

    phi_all = ph[...].reshape(256, 512)
    hgrad = lax.dot_general(phi_all, sg[...].reshape(256, 512), (((1,), (1,)), ((), ())), preferred_element_type=F32)
    pgrad = hgrad * gd[...]
    bias_grad = jnp.sum(pgrad, axis=0, keepdims=True)
    plow = pgrad.astype(BF16)
    phit = phi_all.T
    bias_rows = jnp.broadcast_to(bias_grad, (16, 256)).astype(BF16)
    second_grad = dot(phit, hid[...]).astype(BF16)
    for yy in range(4):
        for hh in range(2):
            q = 2 * yy + hh
            grad = dot(gt[q], plow).astype(BF16)
            tt[yy, hh] = grad[0:192]
            rest = jnp.concatenate([grad[192:256], second_grad[64 * q:64 * q + 64], bias_rows], axis=0)
            tb[0, hh, yy] = rest[:, :128]
            tb[1, hh, yy] = rest[:, 128:]

    def to_units(source, target, first):
        for j in range(2):
            for hh in range(2):
                sid = new("s")
                mine = jnp.logical_and(x == 2 * k + j, k == hh)
                src, dst, rid = source.at[j, hh], target.at[x], first + x
                x_sends.append((src, sid, mine))

                @pl.when(mine)
                def _():
                    pltpu.make_async_copy(src, dst, rsem.at[rid]).start()

                @pl.when(jnp.logical_not(mine))
                def _():
                    remote(src, dst, dev(xx=2 * k + j, kk=hh), sid, rid).start()

    def wait_units(ref, first):
        for j in range(4):
            pltpu.make_async_copy(ref.at[j], ref.at[j], rsem.at[first + j]).wait()

    x_sends = []
    r_vb = new("r", 4)
    to_units(tb, vb, r_vb)
    r_t = new("r", 4)
    for e in (2, 1, 3):
        send(tt.at[plus(y, e)], tr.at[y], dev(yy=plus(y, e)), r_t + y)
    tr[y] = tt[y]
    wait_units(vb, r_vb)
    s = (vb[0].astype(F32) + vb[1].astype(F32)) + (vb[2].astype(F32) + vb[3].astype(F32))
    ub[...] = s.astype(BF16)
    r_w2 = new("r", 4)
    for e in (2, 1, 3):
        send(ub.at[plus(y, e)], yb.at[y], dev(yy=plus(y, e)), r_w2 + y)
    yb[y] = ub[y]

    center_sum(2)
    center_sum(3)

    wait_slots(tr, r_t, y)
    for hh in range(2):
        s = (tr[0, hh].astype(F32) + tr[1, hh].astype(F32)) + (tr[2, hh].astype(F32) + tr[3, hh].astype(F32))
        low = s.astype(BF16)
        u[0, hh] = low[:, :128]
        u[1, hh] = low[:, 128:]
    r_v = new("r", 4)
    to_units(u, v, r_v)

    c_cfh.wait_recv()
    o_coef[y] = (cfh[...].astype(F32) + cfhr[...].astype(F32)).astype(BF16)
    r_o = new("r", 4)
    for e in (1, 3, 2):
        send(o_coef.at[y], o_coef.at[y], dev(yy=plus(y, e)), r_o + y)

    wait_slots(yb, r_w2, y)
    s = (yb[0].astype(F32) + yb[1].astype(F32)) + (yb[2].astype(F32) + yb[3].astype(F32))
    mix[192:336] = s
    mix[336:384] = jnp.zeros((48, 128), F32)
    wait_units(v, r_v)
    mix[0:192] = (v[0].astype(F32) + v[1].astype(F32)) + (v[2].astype(F32) + v[3].astype(F32))
    hs[...] = mix[...].T.astype(BF16).reshape(2, 64, 384)
    s_across, s_also, r_across, s_last, r_last = new("s"), new("s"), new("r"), new("s"), new("r")

    @pl.when(k != h)
    def _():
        remote(hs.at[k], hb, dev(hh=1 - h, kk=k), s_across, r_across).start()
        remote(hs.at[1 - k], hb, dev(hh=1 - h, kk=1 - k), s_also, r_across).start()

    @pl.when(k == h)
    def _():
        remote(hs.at[1 - k], ha, sib, s_last, r_last).start()

    for t in range(4):
        c_ch[t].wait_recv()
        o_cg[:, t * 512:t * 512 + 512] += cghr[t].astype(F32)

    @pl.when(k == h)
    def _():
        ha[...] = hs[k]

    @pl.when(k != h)
    def _():
        pltpu.make_async_copy(ha, ha, rsem.at[r_last]).wait()

    pltpu.make_async_copy(hb, hb, rsem.at[r_across]).wait()
    tot = ha[...].astype(F32) + hb[...].astype(F32)
    o_first[...] = tot[:, 0:256]
    o_second[...] = tot[:, 256:320]
    o_bias[...] = tot[:, 256:384].T[64:65]
    wait_slots(o_coef, r_o, y)

    for cp in sent:
        cp.wait_send()
    for src, dst, sid in homes:
        @pl.when(k != x // 2)
        def _():
            pltpu.make_async_copy(src, src, ssem.at[sid]).wait()
    for src, sid, mine in x_sends:
        @pl.when(jnp.logical_not(mine))
        def _():
            pltpu.make_async_copy(src, src, ssem.at[sid]).wait()

    @pl.when(k != h)
    def _():
        pltpu.make_async_copy(ha, ha, ssem.at[s_across]).wait()
        pltpu.make_async_copy(ha, ha, ssem.at[s_also]).wait()

    @pl.when(k == h)
    def _():
        pltpu.make_async_copy(ha, ha, ssem.at[s_last]).wait()


SCRATCH = (
    ("embt", (64, 1024), BF16), ("w1t", (64, 1024), BF16), ("ctr", (2048, 512), BF16), ("coeft", (100, 2048), BF16), ("cott_in", (100, 1024), BF16),
    ("emb_sib", (64, 1024), BF16), ("emb_all", (4, 4, 2, 32, 128), BF16), ("w_sib", (64, 1024), BF16),
    ("w_pair", (2, 512, 128), BF16), ("b_mine", (8, 128), F32), ("b_sib", (8, 128), F32), ("b_pair", (8, 128), F32),
    ("wg", (2, 4, 512, 128), BF16), ("sg", (2, 2, 64, 512), BF16), ("bg", (2, 2, 8, 128), F32),
    ("g", (4, 4, 2, 4, 32, 128), BF16), ("gt", (8, 256, 256), BF16),
    ("hid", (256, 256), BF16), ("gd", (256, 256), F32),
    ("part", (2, 128, 512), F32), ("part_in", (128, 512), F32),
    ("zs", (4, 32, 512), BF16), ("zown", (4, 32, 512), F32), ("zr", (3, 32, 512), BF16), ("sq", (32, 512), F32),
    ("f", (4, 2, 4, 32, 512), BF16), ("ft", (512, 1024), BF16), ("ct", (4, 512, 512), BF16),
    ("qp", (2048, 128), BF16), ("qt", (4, 128, 512), BF16), ("cn", (4, 8, 512), F32),
    ("cot_pad", (128, 1024), BF16), ("cot_all", (4, 4, 2, 32, 128), BF16), ("cotp", (4, 256, 128), BF16), ("cott", (4, 128, 256), BF16),
    ("kg", (4, 4, 256, 512), F32), ("kb", (4, 1024, 512), BF16), ("wb", (4, 1024, 512), BF16),
    ("rs", (4, 256, 128), F32), ("cs", (4, 8, 512), F32),
    ("rp", (4, 2, 128, 640), BF16), ("prv", (4, 128, 640), BF16), ("xown", (128, 640), F32),
    ("xs_out", (3, 128, 640), BF16), ("xr", (3, 128, 640), BF16),
    ("z2", (4, 32, 640), BF16), ("z2own", (4, 32, 640), F32), ("z2r", (3, 32, 640), BF16), ("ph", (2, 4, 32, 512), BF16),
    ("cgs", (4, 4, 128, 512), BF16), ("cgr", (3, 4, 128, 512), BF16), ("cgh", (4, 2, 64, 512), BF16), ("cghr", (4, 64, 512), BF16),
    ("cfs", (4, 112, 512), BF16), ("cfr", (4, 112, 512), BF16), ("cfh", (112, 512), BF16), ("cfhr", (112, 512), BF16),
    ("tt", (4, 2, 192, 256), BF16), ("tr", (4, 2, 192, 256), BF16), ("u", (2, 2, 192, 128), BF16), ("v", (4, 192, 128), BF16),
    ("tb", (2, 2, 4, 144, 128), BF16), ("vb", (4, 4, 144, 128), BF16), ("ub", (4, 144, 128), BF16), ("yb", (4, 144, 128), BF16),
    ("mix", (384, 128), F32), ("hs", (2, 64, 384), BF16), ("ha", (64, 384), BF16), ("hb", (64, 384), BF16),
)


def finish(pred, first, second, bias, cg, coef, o_pred, o_first, o_second, o_bias, o_cg, o_coef):
    o_pred[...] = pred[...]
    o_first[...] = first[...]
    o_second[...] = second[...]
    o_bias[...] = bias[...]
    o_cg[...] = cg[...]
    for t in range(4):
        o_coef[:, t * 512:t * 512 + 512] = coef[t, 0:100].astype(F32)


def body(embeddings, first_weight, first_bias, second_weight, centers, coefficients, cotangent):
    args = (
        embeddings.T,
        first_weight.T,
        first_bias.reshape(1, 64),
        second_weight,
        centers,
        coefficients.T,
        cotangent.T,
    )
    vmem = pl.BlockSpec(memory_space=pltpu.VMEM)
    anywhere = pl.BlockSpec(memory_space=pl.ANY)
    outs = (
        jax.ShapeDtypeStruct((32, 100), F32),
        jax.ShapeDtypeStruct((64, 256), F32),
        jax.ShapeDtypeStruct((64, 64), F32),
        jax.ShapeDtypeStruct((1, 64), F32),
        jax.ShapeDtypeStruct((64, 2048), F32),
        jax.ShapeDtypeStruct((4, 112, 512), BF16),
    )
    made = pl.pallas_call(
        kernel,
        out_shape=outs,
        in_specs=[anywhere, anywhere, vmem, anywhere, anywhere, anywhere, anywhere],
        out_specs=[vmem] * len(outs),
        scratch_shapes=[pltpu.VMEM(shape, dtype) for name, shape, dtype in SCRATCH]
        + [pltpu.SemaphoreType.DMA((SEMS,)), pltpu.SemaphoreType.DMA((SEMS,))],
        compiler_params=pltpu.CompilerParams(collective_id=0, has_side_effects=True, vmem_limit_bytes=60 << 20),
        name="layer",
    )(*args)
    predictions, grad_first, grad_second, grad_bias, grad_centers, grad_coefs = pl.pallas_call(
        finish,
        out_shape=outs[:5] + (jax.ShapeDtypeStruct((100, 2048), F32),),
        in_specs=[vmem] * len(outs),
        out_specs=[vmem] * len(outs),
        name="finish",
    )(*made)
    return (predictions, grad_first.T, grad_bias[0], grad_second, grad_centers.T, grad_coefs.T)


def solution(mesh):
    placed = (
        P("dp", "center"),
        P(None, "center"),
        P("center"),
        P("center", None),
        P("center", None),
        P("center", None),
        P("dp", None),
    )
    return jax.shard_map(
        body,
        mesh=mesh,
        in_specs=placed,
        out_specs=(
            P(("dp", "center"), None),
            P("dp", "center"),
            P("center"),
            P("center", "dp"),
            P("center", "dp"),
            P("center", None),
        ),
        check_vma=False,
    )
```

time: 143 us -> 117 us (0.82)
  local copies, waits for them, and re-layouts: 17.3 us -> 0 us
  Pallas kernels: 123 us -> 117 us
    unnamed x11 -> x0, local copies, waits for them, and re-layouts: 12.5 us -> none
    pallas_call x1 -> x2, Pallas kernels: 123 us -> 117 us  [the longest x1 114 us: body(): pl.pallas_call(kernel, out_shape=outs, in_specs=[anywhere, anywhere, vmem...]
    reshape x1 -> x0, local copies, waits for them, and re-layouts: 1.87 us -> none  [body(): grad_centers.transpose(0, 2, 1).reshape(2048, 64)]
where the time goes in v2:
time: 117 us
  Pallas kernels  117 us (100%)
    pallas_call x1, Pallas kernels, body(): pl.pallas_call(kernel, out_shape=outs, in_specs=[anywhere, anywhere, vmem...  114 us
    pallas_call x1, Pallas kernels, body(): pl.pallas_call(finish, out_shape=outs[:5] + (jax.ShapeDtypeStruct((100, 2...  2.38 us

profile of v2, /device:TPU:1, one launch (start us, length us, event | category | flops | bytes accessed | tf_op | source)
XLA Modules:
  0.0 117.3 jit_solution(7142612705195060292)
XLA Ops:
  0.6 114.3 %layer.1 = (f32[32,100]{1,0:T(8,128)}, f32[64,256]{1,0:T(8,128)}, f32[64,64]{1,0:T(8,128)}, f32[1,64]{1,0:T(1,128)}, f32[64,2048]{1,0:T(8,128)}, /*index=5*/bf16[4,112,512]{2,1,0:T(8,128)(2,1)}) custom-call(bf16[64,1024]{1,0:T(8,128)(2,1)} %bitcast.12, bf16[64,2048]{1,0:T(8,128)(2,1)} %bitcast.10, f32[1,64]{1,0:T(1,128)} %bitcast.13, bf16[64,512]{1,0:T(8,128)(2,1)} %w2.1, ...), custom_call_target="tpu_custom_call" | custom-call | tf_op jit(solution)/shard_map/layer/pallas_call | solution.py:556
  114.9 2.4 %finish.1 = (f32[32,100]{1,0:T(8,128)}, f32[64,256]{1,0:T(8,128)}, f32[64,64]{1,0:T(8,128)}, f32[1,64]{1,0:T(1,128)}, f32[64,2048]{1,0:T(8,128)}, /*index=5*/f32[100,2048]{1,0:T(8,128)}) custom-call(f32[32,100]{1,0:T(8,128)} %get-tuple-element.18.pred, f32[64,256]{1,0:T(8,128)} %get-tuple-element.19.first, f32[64,64]{1,0:T(8,128)} %get-tuple-element.20.second, ...), custom_call_target="tpu_custom_call" | custom-call | tf_op jit(solution)/shard_map/finish/pallas_call | solution.py:566

commit v3 on v2

--- a/solution.py
+++ b/solution.py
@@ -27,7 +27,7 @@
            hid, gd, part, part_in, zs, zown, zr, sq, f, ft, ct,
            qp, qt, cn, cot_pad, cot_all, cotp, cott, kg, kb, wb,
            rs, cs, rp, prv, xown, xs_out, xr, z2, z2own, z2r, ph,
-           cgs, cgr, cgh, cghr, cfs, cfr, cfh, cfhr, tt, tr, u, v, tb, vb, ub, yb, mix, hs, ha, hb,
+           cgs, cgr, cgh, cghr, cfs, cfr, cfh, cfo, cfhr, tt, tr, u, v, tb, vb, ub, yb, mix, hs, ha, hb,
            ssem, rsem):
     dp = lax.axis_index("dp")
     c = lax.axis_index("center")
@@ -357,10 +357,6 @@
     phi = (total[:, :512] * (1.0 - sq[...] * sq[...])).astype(BF16)
     ph[k, zl] = phi
     c_ph = {e: send(ph.at[k, zl], ph.at[k, zl], dev(zz=plus(zl, e))) for e in (1, 3, 2)}
-    wait_slots(cfr, r_cf, y)
-    s = (cfr[0].astype(F32) + cfr[1].astype(F32)) + (cfr[2].astype(F32) + cfr[3].astype(F32))
-    cfh[...] = s.astype(BF16)
-    c_cfh = send(cfh, cfhr, dev(hh=1 - h))
     c_phs = []
     for e in ORDER:
         if e:
@@ -414,6 +410,10 @@
     for e in (2, 1, 3):
         send(tt.at[plus(y, e)], tr.at[y], dev(yy=plus(y, e)), r_t + y)
     tr[y] = tt[y]
+    wait_slots(cfr, r_cf, y)
+    s = (cfr[0].astype(F32) + cfr[1].astype(F32)) + (cfr[2].astype(F32) + cfr[3].astype(F32))
+    cfh[...] = s.astype(BF16)
+    c_cfh = send(cfh, cfhr, dev(hh=1 - h))
     wait_units(vb, r_vb)
     s = (vb[0].astype(F32) + vb[1].astype(F32)) + (vb[2].astype(F32) + vb[3].astype(F32))
     ub[...] = s.astype(BF16)
@@ -435,10 +435,10 @@
     to_units(u, v, r_v)
 
     c_cfh.wait_recv()
-    o_coef[y] = (cfh[...].astype(F32) + cfhr[...].astype(F32)).astype(BF16)
+    cfo[y] = (cfh[...].astype(F32) + cfhr[...].astype(F32)).astype(BF16)
     r_o = new("r", 4)
     for e in (1, 3, 2):
-        send(o_coef.at[y], o_coef.at[y], dev(yy=plus(y, e)), r_o + y)
+        send(cfo.at[y], cfo.at[y], dev(yy=plus(y, e)), r_o + y)
 
     wait_slots(yb, r_w2, y)
     s = (yb[0].astype(F32) + yb[1].astype(F32)) + (yb[2].astype(F32) + yb[3].astype(F32))
@@ -462,6 +462,10 @@
         c_ch[t].wait_recv()
         o_cg[:, t * 512:t * 512 + 512] += cghr[t].astype(F32)
 
+    wait_slots(cfo, r_o, y)
+    for t in range(4):
+        o_coef[:, t * 512:t * 512 + 512] = cfo[t, 0:100].astype(F32)
+
     @pl.when(k == h)
     def _():
         ha[...] = hs[k]
@@ -475,7 +479,6 @@
     o_first[...] = tot[:, 0:256]
     o_second[...] = tot[:, 256:320]
     o_bias[...] = tot[:, 256:384].T[64:65]
-    wait_slots(o_coef, r_o, y)
 
     for cp in sent:
         cp.wait_send()
@@ -516,21 +519,17 @@
     ("xs_out", (3, 128, 640), BF16), ("xr", (3, 128, 640), BF16),
     ("z2", (4, 32, 640), BF16), ("z2own", (4, 32, 640), F32), ("z2r", (3, 32, 640), BF16), ("ph", (2, 4, 32, 512), BF16),
     ("cgs", (4, 4, 128, 512), BF16), ("cgr", (3, 4, 128, 512), BF16), ("cgh", (4, 2, 64, 512), BF16), ("cghr", (4, 64, 512), BF16),
-    ("cfs", (4, 112, 512), BF16), ("cfr", (4, 112, 512), BF16), ("cfh", (112, 512), BF16), ("cfhr", (112, 512), BF16),
+    ("cfs", (4, 112, 512), BF16), ("cfr", (4, 112, 512), BF16), ("cfh", (112, 512), BF16), ("cfo", (4, 112, 512), BF16), ("cfhr", (112, 512), BF16),
     ("tt", (4, 2, 192, 256), BF16), ("tr", (4, 2, 192, 256), BF16), ("u", (2, 2, 192, 128), BF16), ("v", (4, 192, 128), BF16),
     ("tb", (2, 2, 4, 144, 128), BF16), ("vb", (4, 4, 144, 128), BF16), ("ub", (4, 144, 128), BF16), ("yb", (4, 144, 128), BF16),
     ("mix", (384, 128), F32), ("hs", (2, 64, 384), BF16), ("ha", (64, 384), BF16), ("hb", (64, 384), BF16),
 )
 
 
-def finish(pred, first, second, bias, cg, coef, o_pred, o_first, o_second, o_bias, o_cg, o_coef):
-    o_pred[...] = pred[...]
-    o_first[...] = first[...]
-    o_second[...] = second[...]
-    o_bias[...] = bias[...]
-    o_cg[...] = cg[...]
-    for t in range(4):
-        o_coef[:, t * 512:t * 512 + 512] = coef[t, 0:100].astype(F32)
+def finish(*refs):
+    n = len(refs) // 2
+    for i in range(n):
+        refs[n + i][...] = refs[i][...]
 
 
 def body(embeddings, first_weight, first_bias, second_weight, centers, coefficients, cotangent):
@@ -551,7 +550,7 @@
         jax.ShapeDtypeStruct((64, 64), F32),
         jax.ShapeDtypeStruct((1, 64), F32),
         jax.ShapeDtypeStruct((64, 2048), F32),
-        jax.ShapeDtypeStruct((4, 112, 512), BF16),
+        jax.ShapeDtypeStruct((100, 2048), F32),
     )
     made = pl.pallas_call(
         kernel,
@@ -565,7 +564,7 @@
     )(*args)
     predictions, grad_first, grad_second, grad_bias, grad_centers, grad_coefs = pl.pallas_call(
         finish,
-        out_shape=outs[:5] + (jax.ShapeDtypeStruct((100, 2048), F32),),
+        out_shape=outs,
         in_specs=[vmem] * len(outs),
         out_specs=[vmem] * len(outs),
         name="finish",

time: 117 us -> 112 us (0.957)
  Pallas kernels: 117 us -> 111 us
    pallas_call x1, Pallas kernels: 114 us -> 109 us  [body(): pl.pallas_call(kernel, out_shape=outs, in_specs=[anywhere, anywhere, vmem...]
where the time goes in v3:
time: 112 us
  Pallas kernels  111 us (99%)
    pallas_call x1, Pallas kernels, body(): pl.pallas_call(kernel, out_shape=outs, in_specs=[anywhere, anywhere, vmem...  109 us
    pallas_call x1, Pallas kernels, body(): pl.pallas_call(finish, out_shape=outs, in_specs=[vmem] * len(outs), out_s...  2.52 us

profile of v3, /device:TPU:1, one launch (start us, length us, event | category | flops | bytes accessed | tf_op | source)
XLA Modules:
  0.0 111.9 jit_solution(17771544880552884411)
XLA Ops:
  0.6 108.7 %layer.1 = (f32[32,100]{1,0:T(8,128)}, f32[64,256]{1,0:T(8,128)}, f32[64,64]{1,0:T(8,128)}, f32[1,64]{1,0:T(1,128)}, f32[64,2048]{1,0:T(8,128)}, /*index=5*/f32[100,2048]{1,0:T(8,128)}) custom-call(bf16[64,1024]{1,0:T(8,128)(2,1)} %bitcast.12, bf16[64,2048]{1,0:T(8,128)(2,1)} %bitcast.10, f32[1,64]{1,0:T(1,128)} %bitcast.13, bf16[64,512]{1,0:T(8,128)(2,1)} %w2.1, ...), custom_call_target="tpu_custom_call" | custom-call | tf_op jit(solution)/shard_map/layer/pallas_call | solution.py:555
  109.4 2.5 %finish.1 = (f32[32,100]{1,0:T(8,128)}, f32[64,256]{1,0:T(8,128)}, f32[64,64]{1,0:T(8,128)}, f32[1,64]{1,0:T(1,128)}, f32[64,2048]{1,0:T(8,128)}, /*index=5*/f32[100,2048]{1,0:T(8,128)}) custom-call(f32[32,100]{1,0:T(8,128)} %get-tuple-element.18.refs_0_, f32[64,256]{1,0:T(8,128)} %get-tuple-element.19.refs_1_, f32[64,64]{1,0:T(8,128)} %get-tuple-element.20.refs_2_, ...), custom_call_target="tpu_custom_call" | custom-call | tf_op jit(solution)/shard_map/finish/pallas_call | solution.py:565

commit v4 on v3

--- a/solution.py
+++ b/solution.py
@@ -318,7 +318,11 @@
         ft[:, 256 * i:256 * i + 256] = f[minus(x, d)].reshape(256, 512).T
         if i < 3:
             weigh(i, 0, 2)
-            forward(ORDER[i + 1])
+        if i == 0:
+            forward(1)
+            forward(3)
+        if i == 1:
+            forward(2)
     weigh(3, 0, 1)
     center_out(0)
     weigh(3, 1, 2)

time: 112 us -> 111 us (level)
    pallas_call x1, Pallas kernels: 109 us -> 107 us  [body(): pl.pallas_call(kernel, out_shape=outs, in_specs=[anywhere, anywhere, vmem...]
where the time goes in v4:
time: 111 us; the launch traced here: 110 us
  Pallas kernels  110 us (99%)
    pallas_call x1, Pallas kernels, body(): pl.pallas_call(kernel, out_shape=outs, in_specs=[anywhere, anywhere, vmem...  107 us
    pallas_call x1, Pallas kernels, body(): pl.pallas_call(finish, out_shape=outs, in_specs=[vmem] * len(outs), out_s...  2.52 us

profile of v4, /device:TPU:1, one launch (start us, length us, event | category | flops | bytes accessed | tf_op | source)
XLA Modules:
  0.0 110.4 jit_solution(1579800019832488221)
XLA Ops:
  0.6 107.2 %layer.1 = (f32[32,100]{1,0:T(8,128)}, f32[64,256]{1,0:T(8,128)}, f32[64,64]{1,0:T(8,128)}, f32[1,64]{1,0:T(1,128)}, f32[64,2048]{1,0:T(8,128)}, /*index=5*/f32[100,2048]{1,0:T(8,128)}) custom-call(bf16[64,1024]{1,0:T(8,128)(2,1)} %bitcast.12, bf16[64,2048]{1,0:T(8,128)(2,1)} %bitcast.10, f32[1,64]{1,0:T(1,128)} %bitcast.13, bf16[64,512]{1,0:T(8,128)(2,1)} %w2.1, ...), custom_call_target="tpu_custom_call" | custom-call | tf_op jit(solution)/shard_map/layer/pallas_call | solution.py:559
  107.9 2.5 %finish.1 = (f32[32,100]{1,0:T(8,128)}, f32[64,256]{1,0:T(8,128)}, f32[64,64]{1,0:T(8,128)}, f32[1,64]{1,0:T(1,128)}, f32[64,2048]{1,0:T(8,128)}, /*index=5*/f32[100,2048]{1,0:T(8,128)}) custom-call(f32[32,100]{1,0:T(8,128)} %get-tuple-element.18.refs_0_, f32[64,256]{1,0:T(8,128)} %get-tuple-element.19.refs_1_, f32[64,64]{1,0:T(8,128)} %get-tuple-element.20.refs_2_, ...), custom_call_target="tpu_custom_call" | custom-call | tf_op jit(solution)/shard_map/finish/pallas_call | solution.py:569
